TPU v7x, 128 devices: a whole 4x4x4 slice. The times are simulated.
128 devices in a mesh: section: 2 (over x_hi), group: 16 (over z, y), replica: 4 (over x_lo, core).
Axes of the slice: x: 4 (x_hi: 2, x_lo: 2; x = x_hi * 2 + x_lo), y: 4, z: 4, core: 2. Of those that a mesh axis runs over, the one named last changes fastest.
Arguments:
- inputs: bfloat16 [4, 2, 1024, 896], P('replica', None, 'group'), may hold values from -6 to 6
- cotangent: bfloat16 [4, 2, 1024, 896], P('replica', None, 'group'), may hold values from -6 to 6
- segments: int32 [4, 2048], P('replica'), may hold values from 0 to 6, as said below
- w_qkv: bfloat16 [2, 896, 1152], P('section', 'group'), may hold values from -0.1875 to 0.1875
- b_qkv: bfloat16 [2, 1152], P('section', 'group'), may hold values from -3 to 3
- w_out: bfloat16 [2, 896, 896], P('section', 'group'), may hold values from -1.5 to 1.5
- w_gate: bfloat16 [2, 896, 4864], P('section', 'group'), may hold values from -0.1875 to 0.1875
- w_up: bfloat16 [2, 896, 4864], P('section', 'group'), may hold values from -0.1875 to 0.1875
- w_down: bfloat16 [2, 4864, 896], P('section', 'group'), may hold values from -0.15625 to 0.15625
- g_attn: bfloat16 [2, 896], P('section', 'group'), may hold values from 0.5 to 1.5
- g_mlp: bfloat16 [2, 896], P('section', 'group'), may hold values from 0.5 to 1.5
Outputs:
- block_out: bfloat16 [2, 4, 2, 1024, 896], P('section', 'replica', None, 'group')
- input_grad: bfloat16 [2, 4, 2, 1024, 896], P('section', 'replica', None, 'group')
- grad_qkv: float32 [2, 896, 1152], P('section', 'group')
- grad_bias: float32 [2, 1024], P('section', 'group')
- grad_value_bias: float32 [2, 128], P('section', 'group')
- grad_out: float32 [2, 896, 896], P('section', 'group')
- grad_gate: float32 [2, 896, 4864], P('section', 'group')
- grad_up: float32 [2, 896, 4864], P('section', 'group')
- grad_down: float32 [2, 4864, 896], P('section', 'group')
- grad_attn_gain: float32 [2, 896], P('section', 'group')
- grad_mlp_gain: float32 [2, 896], P('section', 'group')
Inputs may be any that keep to these rules, and one draw needn't show every extreme that they name: `segments`: document numbers never fall along a sequence, and the last token of every sequence carries the largest; in each sequence one document covers a whole block of 1024 tokens that starts at a multiple of 1024.
All inputs are finite; a program needn't handle non-finite values.
Results may differ from a plain program's by a relative error of at most 0.035.
Values may be sent and summed in bfloat16 or wider, within the bound.
A program may use at most 192 MiB of HBM per device.

v0:
```python
import functools

import jax
import jax.numpy as jnp
import numpy as np
from jax import lax
from jax.experimental import pallas as pl
from jax.experimental.pallas import tpu as pltpu
from jax.sharding import PartitionSpec as P

D = 896
HEADS = 14
KV = 128
HALF = 32
FF = 4864
QUARTER = FF // 4
QKV = 1152
ROWS = 128
SPAN = 1024
LEN = 2048
PAIRS = 7
EPSILON = 1e-06
THETA = 1000000.0
NEGATIVE = -1e30
SCALE = 0.125
VMEM_LIMIT = 60 * 1024 * 1024
MESH = pl.DeviceIdType.MESH
BF = jnp.bfloat16
F32 = jnp.float32
VMEM_SPEC = pl.BlockSpec(memory_space=pltpu.VMEM)
ANY_SPEC = pl.BlockSpec(memory_space=pl.ANY)


def nn(a, b):
    return lax.dot_general(a, b, (((1,), (0,)), ((), ())), preferred_element_type=F32)


def nt(a, b):
    return lax.dot_general(a, b, (((1,), (1,)), ((), ())), preferred_element_type=F32)


def tn(a, b):
    return lax.dot_general(a, b, (((0,), (0,)), ((), ())), preferred_element_type=F32)


def params(collective_id=None):
    if collective_id is None:
        return pltpu.CompilerParams(vmem_limit_bytes=VMEM_LIMIT)
    return pltpu.CompilerParams(
        vmem_limit_bytes=VMEM_LIMIT, collective_id=collective_id, has_side_effects=True
    )


def shaped(*shape, dtype=BF):
    return jax.ShapeDtypeStruct(shape, dtype)


def local_call(kernel, name, out_shape, scratch=()):
    return pl.pallas_call(
        kernel,
        out_shape=out_shape,
        scratch_shapes=list(scratch),
        compiler_params=params(),
        name=name,
    )


def signal(devices):
    barrier = pltpu.get_barrier_semaphore()
    for device in devices:
        pl.semaphore_signal(barrier, inc=1, device_id=device, device_id_type=MESH)


def greeted(count):
    pl.semaphore_wait(pltpu.get_barrier_semaphore(), count)


def grid_place():
    me = lax.axis_index("group")
    z = me // 4
    y = lax.rem(me, 4)

    def along_y(step):
        return {"group": z * 4 + lax.rem(y + step, 4)}

    def along_z(step):
        return {"group": lax.rem(z + step, 4) * 4 + y}

    return z, y, along_y, along_z


def neighbours(along_y, along_z):
    return [along_y(1), along_y(3), along_z(1), along_z(3)]


class Copies:
    def __init__(self, send, recv):
        self.send, self.recv, self.used = send, recv, 0

    def __call__(self, src, dst, device, start=True):
        index = self.used
        self.used += 1
        each = pltpu.make_async_remote_copy(
            src_ref=src,
            dst_ref=dst,
            send_sem=self.send.at[index],
            recv_sem=self.recv.at[index],
            device_id=device,
            device_id_type=MESH,
        )
        if start:
            each.start()
        return each


def gather_phase(firsts, seconds, place, device_at, copies):
    def copy(block, slot, step):
        return copies(block(slot), block(slot), device_at(step), False)

    firsts_right = [copy(block, place, 1) for block in firsts]
    seconds_left = [copy(block, place, 3) for block in seconds]
    others = [copy(block, place, 3) for block in firsts] + [copy(block, place, 1) for block in seconds]
    relays = [copy(block, lax.rem(place + 3, 4), 1) for block in firsts]
    relays += [copy(block, lax.rem(place + 1, 4), 3) for block in seconds]

    def start():
        for each in firsts_right + seconds_left + others:
            each.start()

    def relay():
        for came, each in zip(firsts_right + seconds_left, relays):
            came.wait_recv()
            each.start()

    def finish():
        for each in others + relays:
            each.wait_recv()
        for each in firsts_right + seconds_left + others + relays:
            each.wait_send()

    return start, relay, finish


def gather_both(first_a, second_a, first_b, second_b, copies):
    z, y, along_y, along_z = grid_place()
    start_a, relay_a, finish_a = gather_phase([first_a[0]], [second_a[0]], y, along_y, copies)
    start_b, relay_b, finish_b = gather_phase([first_b[0]], [second_b[0]], z, along_z, copies)
    then_a, last_a, end_a = gather_phase([first_a[1]], [second_a[1]], z, along_z, copies)
    then_b, last_b, end_b = gather_phase([first_b[1]], [second_b[1]], y, along_y, copies)
    start_a()
    start_b()
    yield
    relay_a()
    relay_b()
    yield
    finish_a()
    then_a()
    finish_b()
    then_b()
    yield
    last_a()
    last_b()
    yield
    end_a()
    end_b()


def gather_split(first_a, second_a, first_b, second_b, copies):
    z, y, along_y, along_z = grid_place()
    slim = [
        gather_phase([first_a[0]], [second_a[0]], y, along_y, copies),
        gather_phase([first_b[0]], [second_b[0]], z, along_z, copies),
    ]

    def wide(half):
        def part(function):
            return [lambda at: function(at, half)]

        return [
            gather_phase(part(first_a[1]), part(second_a[1]), z, along_z, copies),
            gather_phase(part(first_b[1]), part(second_b[1]), y, along_y, copies),
        ]

    halves = [wide(slice(0, 2)), wide(slice(2, 4))]
    for start, _, _ in slim:
        start()
    yield
    for _, relay, _ in slim:
        relay()
    yield
    for _, _, finish in slim:
        finish()
    for phases in halves:
        for start, _, _ in phases:
            start()
        yield
        for _, relay, _ in phases:
            relay()
        yield
    for phases in halves:
        for _, _, finish in phases:
            finish()


def run(steps):
    for _ in steps:
        pass


def y_then_z(ref, *tail):
    z = lax.axis_index("group") // 4
    return (lambda at: ref.at[(z, at, *tail)]), (lambda at, part=slice(None): ref.at[(at, part, *tail)])


def z_then_y(ref, *tail):
    y = lax.rem(lax.axis_index("group"), 4)
    return (lambda at: ref.at[(at, y, *tail)]), (lambda at, part=slice(None): ref.at[(part, at, *tail)])


def quarter_route():
    group, replica = lax.axis_index("group"), lax.axis_index("replica")
    target = {"group": 4 * lax.rem(group, 4) + replica, "replica": group // 4}
    source = {"group": 4 * replica + group // 4, "replica": lax.rem(group, 4)}
    stays = (target["group"] == group) & (target["replica"] == replica)
    return target, source, stays


def first_kernel(
    gate, up, down, qkv, out, x_ref, cos_ref, sin_ref, kseg_ref,
    gate_all, up_all, down_all, qkv_w, out_w, bias_ref, gain1_ref, gain2_ref, hidden_ref, normed2_ref,
    qkv_all, out_all, normed_ref, q_ref, kv_ref, context_ref, keys_ref, values_ref, bias0, bias1, send, recv, local
):
    z, y, along_y, along_z = grid_place()
    core = lax.rem(lax.axis_index("replica"), 2)
    mate = {"replica": lax.axis_index("replica") + 1 - 2 * core}
    target, source, stays = quarter_route()
    moves = jnp.logical_not(stays)
    signal(neighbours(along_y, along_z) + [mate])
    places = (qkv_all.at[core, z, y], out_all.at[core, z, y], gate_all.at[z, y], up_all.at[z, y])
    own = []
    for index, (src, dst) in enumerate(zip((qkv, out, gate, up), places)):
        own.append(pltpu.make_async_copy(src, dst, local.at[index]))
        own[-1].start()
    there = target["group"]
    moved = pltpu.make_async_remote_copy(
        src_ref=down,
        dst_ref=down_all.at[there // 4, lax.rem(there, 4)],
        send_sem=local.at[5],
        recv_sem=local.at[6],
        device_id=target,
        device_id_type=MESH,
    )
    stayed = pltpu.make_async_copy(down, down_all.at[z, y], local.at[4])

    @pl.when(moves)
    def _():
        signal([source])
        greeted(6)
        moved.start()

    @pl.when(stays)
    def _():
        greeted(5)
        stayed.start()

    copies = Copies(send, recv)
    own[0].wait()
    own[1].wait()
    top, bottom = (slice(0, 16), slice(None)), (slice(16, 32), slice(None))
    dense = gather_both(
        y_then_z(qkv_all.at[core], *top),
        y_then_z(qkv_all.at[core], *bottom),
        z_then_y(out_all.at[core], *top),
        z_then_y(out_all.at[core], *bottom),
        copies,
    )
    next(dense)
    next(dense)
    next(dense)
    own[2].wait()
    own[3].wait()

    @pl.when(moves)
    def _():
        moved.wait()

    @pl.when(stays)
    def _():
        stayed.wait()

    left, right = (slice(None), slice(0, 512)), (slice(None), slice(512, D))
    wide = gather_split(
        y_then_z(gate_all), y_then_z(down_all, *left), z_then_y(up_all), z_then_y(down_all, *right), copies
    )
    next(wide)
    next(dense)
    next(wide)
    run(dense)
    halves = [copies(ref.at[core], ref.at[core], mate) for ref in (qkv_all, out_all)]
    next(wide)
    for each in halves:
        each.wait()
    for at in range(16):
        rows, cut = 56 * at, 56 * at + 32
        qkv_w[rows:cut] = qkv_all[0, at // 4, at % 4]
        qkv_w[cut : rows + 56] = qkv_all[1, at // 4, at % 4, :24]
        out_w[rows:cut] = out_all[0, at // 4, at % 4]
        out_w[cut : rows + 56] = out_all[1, at // 4, at % 4, :24]
    small = [qkv_all[1, at // 4, at % 4, 24:32].astype(F32)[:1] for at in range(16)]
    bias_ref[...] = jnp.concatenate([each[:, :72] for each in small], axis=1)
    gain1_ref[...] = jnp.concatenate([each[:, 72:128] for each in small], axis=1)
    gain2_ref[...] = jnp.concatenate([each[:, 128:184] for each in small], axis=1)
    kv = front_work(x_ref, qkv_w, bias_ref, gain1_ref, cos_ref, sin_ref, normed_ref, q_ref, kv_ref, copies, None)
    next(kv)
    next(wide)
    next(kv)
    next(kv)
    next(wide)
    run(kv)
    attention_work(
        x_ref, q_ref, kv_ref, kseg_ref, out_w, gain2_ref, context_ref, hidden_ref, normed2_ref,
        keys_ref, values_ref, bias0, bias1, lambda: next(wide)
    )
    run(wide)


def first(gate, up, down, qkv, out, x, cosine, sine, kseg):
    return pl.pallas_call(
        first_kernel,
        out_shape=(
            shaped(4, 4, *gate.shape),
            shaped(4, 4, *up.shape),
            shaped(4, 4, *down.shape),
            shaped(D, QKV),
            shaped(D, D),
            shaped(1, QKV, dtype=F32),
            shaped(1, D, dtype=F32),
            shaped(1, D, dtype=F32),
            shaped(ROWS, D, dtype=F32),
            shaped(ROWS, D),
        ),
        in_specs=[ANY_SPEC] * 5 + [VMEM_SPEC] * 4,
        out_specs=[ANY_SPEC] * 3 + [VMEM_SPEC] * 7,
        scratch_shapes=[
            pltpu.VMEM((2, 4, 4, *qkv.shape), BF),
            pltpu.VMEM((2, 4, 4, *out.shape), BF),
            pltpu.VMEM((ROWS, D), BF),
            pltpu.VMEM((ROWS, D), BF),
            pltpu.VMEM((2, 4, 4, 64, 2 * KV), BF),
            pltpu.VMEM((ROWS, D), BF),
        ]
        + ATTENTION_SCRATCH
        + [
            pltpu.SemaphoreType.DMA((86,)),
            pltpu.SemaphoreType.DMA((86,)),
            pltpu.SemaphoreType.DMA((7,)),
        ],
        compiler_params=params(0),
        name="first",
    )(gate, up, down, qkv, out, x, cosine, sine, kseg)


def scatter_phase(firsts, seconds, place, device_at, copies):
    right, left, far = (lax.rem(place + step, 4) for step in (1, 3, 2))

    def load(ref):
        return ref[...].astype(F32)

    def copy(src, dst, step):
        return copies(src, dst, device_at(step), False)

    first_far = [copy(block(far), bufs[0], 1) for block, bufs, put in firsts]
    second_far = [copy(block(far), bufs[0], 3) for block, bufs, put in seconds]
    first_near = [copy(block(left), bufs[2], 3) for block, bufs, put in firsts]
    second_near = [copy(block(right), bufs[1], 1) for block, bufs, put in seconds]
    first_sum = [copy(bufs[0], bufs[1], 1) for block, bufs, put in firsts]
    second_sum = [copy(bufs[0], bufs[2], 3) for block, bufs, put in seconds]

    def start():
        for each in first_far + second_far + first_near + second_near:
            each.start()

    def pass_on():
        for came, each, (block, bufs, put) in zip(first_far, first_sum, firsts):
            came.wait_recv()
            bufs[0][...] = (load(block(right)) + load(bufs[0])).astype(BF)
            each.start()
        for came, each, (block, bufs, put) in zip(second_far, second_sum, seconds):
            came.wait_recv()
            bufs[0][...] = (load(block(left)) + load(bufs[0])).astype(BF)
            each.start()

    def finish():
        near, far_sum = first_near + second_near, first_sum + second_sum
        for one, two, (block, bufs, put) in zip(near, far_sum, firsts + seconds):
            one.wait_recv()
            two.wait_recv()
            put(load(block(place)) + load(bufs[1]) + load(bufs[2]))
        for each in first_far + second_far + near + far_sum:
            each.wait_send()

    return start, pass_on, finish


def scatter_both(first_a, second_a, first_b, second_b, copies):
    z, y, along_y, along_z = grid_place()

    def wide(part):
        block, bufs, _, _ = part
        return [(block, bufs, stored_in(bufs[1]))]

    def slim(part):
        _, kept, bufs, put = part
        return [((lambda at: kept[1].at[at]), bufs, put)]

    start_a, pass_a, finish_a = scatter_phase(wide(first_a), wide(second_a), y, along_y, copies)
    start_b, pass_b, finish_b = scatter_phase(wide(first_b), wide(second_b), z, along_z, copies)
    then_a, last_a, end_a = scatter_phase(slim(first_a), slim(second_a), z, along_z, copies)
    then_b, last_b, end_b = scatter_phase(slim(first_b), slim(second_b), y, along_y, copies)
    start_a()
    start_b()
    yield
    pass_a()
    pass_b()
    yield
    finish_a()
    then_a()
    finish_b()
    then_b()
    yield
    last_a()
    last_b()
    yield
    end_a()
    end_b()


def scatter_split(first_a, second_a, first_b, second_b, copies):
    z, y, along_y, along_z = grid_place()

    def slim(part):
        _, kept, bufs, put = part
        return [((lambda at: kept[1].at[at]), bufs, put)]

    def halved(half):
        def wide(part):
            block, bufs, _, _ = part
            views = [each.at[half] for each in bufs]
            return [(lambda at: block(at, half), views, stored_in(views[1]))]

        return [
            scatter_phase(wide(first_a), wide(second_a), y, along_y, copies),
            scatter_phase(wide(first_b), wide(second_b), z, along_z, copies),
        ]

    halves = [halved(pl.ds(0, 2)), halved(pl.ds(2, 2))]
    last_phases = [
        scatter_phase(slim(first_a), slim(second_a), z, along_z, copies),
        scatter_phase(slim(first_b), slim(second_b), y, along_y, copies),
    ]
    for start, _, _ in halves[0]:
        start()
    yield
    for _, pass_on, _ in halves[0]:
        pass_on()
    for start, _, _ in halves[1]:
        start()
    yield
    for _, pass_on, _ in halves[1]:
        pass_on()
    yield
    for phases in halves:
        for _, _, finish in phases:
            finish()
    for start, _, _ in last_phases:
        start()
    yield
    for _, pass_on, _ in last_phases:
        pass_on()
    yield
    for _, _, finish in last_phases:
        finish()


def scatter_scratch(*shapes):
    scratch = []
    for shape in shapes:
        scratch += [pltpu.VMEM((4, *shape), BF)] * 3 + [pltpu.VMEM(shape, BF)] * 3
    return scratch


def scatter_part(scratch, index, block, put):
    mine = scratch[6 * index : 6 * index + 6]
    return block, mine[:3], mine[3:], put


def stored_in(ref, *at):
    def put(value):
        ref[at if at else ...] = value.astype(ref.dtype)

    return put


DOWN_STARTS = (0, 80, 160, 224)
DOWN_ROWS = 80


def mlp_terms(rows_ref, dgate_ref, dup_ref, product_ref, dout_ref, gate_terms, up_terms, down_terms):
    def flat(ref):
        return ref[...].reshape(4 * ROWS, ref.shape[-1])

    rows = flat(rows_ref)
    for terms, grads in ((gate_terms, dgate_ref), (up_terms, dup_ref)):
        whole = tn(rows, flat(grads))
        for at in range(16):
            terms[at // 4, at % 4] = whole[56 * at : 56 * at + 56].astype(BF)
    whole = tn(flat(product_ref), flat(dout_ref)).astype(BF)
    for at in range(16):
        start = 304 * (at // 4) + DOWN_STARTS[at % 4]
        down_terms[at // 4, at % 4] = whole[start : start + DOWN_ROWS]


def mlp_sums(gate_terms, up_terms, down_terms, gate_out, up_out, down_out, scratch, copies):
    left, right = slice(0, 512), slice(512, D)
    return scatter_split(
        scatter_part(scratch, 0, lambda at, part: gate_terms.at[part, at], stored_in(gate_out)),
        scatter_part(
            scratch, 2, lambda at, part: down_terms.at[part, at, :, left], stored_in(down_out, slice(None), left)
        ),
        scatter_part(scratch, 1, lambda at, part: up_terms.at[at, part], stored_in(up_out)),
        scatter_part(
            scratch, 3, lambda at, part: down_terms.at[at, part, :, right], stored_in(down_out, slice(None), right)
        ),
        copies,
    )


MLP_SUMS_SHAPES = ((56, QUARTER), (56, QUARTER), (DOWN_ROWS, 512), (DOWN_ROWS, D - 512))


def qkv_sums(qkv_half, out_half, qkv_sum, out_sum, scratch, copies):
    top, bottom = slice(0, 16), slice(16, 32)
    return scatter_both(
        scatter_part(scratch, 0, lambda at: qkv_half.at[:, at, top], stored_in(qkv_sum, top)),
        scatter_part(scratch, 1, lambda at: qkv_half.at[:, at, bottom], stored_in(qkv_sum, bottom)),
        scatter_part(scratch, 2, lambda at: out_half.at[at, :, top], stored_in(out_sum, top)),
        scatter_part(scratch, 3, lambda at: out_half.at[at, :, bottom], stored_in(out_sum, bottom)),
        copies,
    )


def kv_sums(dkv_ref, total, scratch, copies):
    top, bottom = slice(0, 32), slice(32, 64)
    return scatter_both(
        scatter_part(scratch, 0, lambda at: dkv_ref.at[0, :, at, top], stored_in(total, slice(0, 32))),
        scatter_part(scratch, 1, lambda at: dkv_ref.at[0, :, at, bottom], stored_in(total, slice(32, 64))),
        scatter_part(scratch, 2, lambda at: dkv_ref.at[1, at, :, top], stored_in(total, slice(64, 96))),
        scatter_part(scratch, 3, lambda at: dkv_ref.at[1, at, :, bottom], stored_in(total, slice(96, 128))),
        copies,
    )


def replica_partners():
    me = lax.axis_index("replica")
    return me, me + 1 - 2 * lax.rem(me, 2), lax.rem(me + 2, 4), 3 - me


def exchange(
    own_ref, all_ref, total_ref, near_terms, part, far_part, near_sum, part_in, far_in, near_in, copies, loads, work
):
    me, mate, next_, far = replica_partners()
    halves = (slice(0, 64), slice(64, 128))
    to_mate, to_next = {"replica": mate}, {"replica": next_}
    greeted(2)
    across = [copies(own_ref.at[half], all_ref.at[me, half], to_next) for half in halves]
    beside = copies(own_ref, all_ref.at[me], to_mate)
    forwards = [copies(all_ref.at[next_, half], all_ref.at[next_, half], to_mate, False) for half in halves]
    passed = [copies(far_part.at[index], far_in.at[index], to_mate, False) for index in (0, 1)]
    sums = [copies(near_sum.at[index], near_in.at[index], to_next, False) for index in (0, 1)]
    sent = copies(part, part_in, to_mate, False)
    all_ref[me] = own_ref[...]
    for each in loads:
        each.wait()

    def send_sum(index):
        passed[index].wait_recv()
        near_sum[index] = (near_terms[index] + far_in[index].astype(F32)).astype(BF)
        sums[index].start()

    def step(at, carry):
        one = jnp.where(at == 0, me, jnp.where(at == 3, mate, next_))
        two = jnp.where(at == 0, me, jnp.where(at == 3, mate, far))
        first_rows = pl.ds(pl.multiple_of(jnp.where(at == 2, 64, 0), 64), 64)
        second_rows = pl.ds(pl.multiple_of(jnp.where(at == 1, 0, 64), 64), 64)

        @pl.when(at == 1)
        def _():
            across[0].wait_recv()
            forwards[0].start()
            forwards[0].wait_recv()

        @pl.when(at == 2)
        def _():
            across[1].wait_recv()
            forwards[1].start()
            send_sum(0)
            forwards[1].wait_recv()

        @pl.when(at == 3)
        def _():
            send_sum(1)
            beside.wait_recv()

        terms = work([(one, first_rows), (two, second_rows)])

        @pl.when(at == 0)
        def _():
            total_ref[...] = terms

        for index in (0, 1):

            @pl.when(at == 1 + index)
            def _(index=index):
                near_terms[index] = terms[:64]
                far_part[index] = terms[64:].astype(BF)
                passed[index].start()

        @pl.when(at == 3)
        def _():
            part[...] = terms.astype(BF)
            sent.start()

        return carry

    lax.fori_loop(0, 4, step, 0)
    sent.wait_recv()
    total = total_ref[...] + part_in[...].astype(F32)
    for each in sums:
        each.wait_recv()
    total = total + near_in[...].reshape(ROWS, D).astype(F32)
    for each in across + [beside, sent] + forwards + passed + sums:
        each.wait_send()
    return total


EXCHANGE_SCRATCH = [
    pltpu.VMEM((D, QUARTER), BF),
    pltpu.VMEM((D, QUARTER), BF),
    pltpu.VMEM((QUARTER, D), BF),
    pltpu.VMEM((ROWS, D), F32),
    pltpu.VMEM((2, 64, D), F32),
    pltpu.VMEM((ROWS, D), BF),
    pltpu.VMEM((2, 64, D), BF),
    pltpu.VMEM((2, 64, D), BF),
    pltpu.VMEM((ROWS, D), BF),
    pltpu.VMEM((2, 64, D), BF),
    pltpu.VMEM((2, 64, D), BF),
    pltpu.SemaphoreType.DMA((10,)),
    pltpu.SemaphoreType.DMA((10,)),
    pltpu.SemaphoreType.DMA((18,)),
]


def mlp_start(hbm, vmem, local):
    me, mate, next_, far = replica_partners()
    signal([{"replica": mate}, {"replica": next_}])
    loads = [pltpu.make_async_copy(src, dst, local.at[i]) for i, (src, dst) in enumerate(zip(hbm[:2], vmem[:2]))]
    for at in range(16):
        skip = 80 * (at % 4) - DOWN_STARTS[at % 4]
        rows = pl.ds(304 * (at // 4) + 80 * (at % 4), DOWN_ROWS - skip)
        piece = hbm[2].at[at // 4, at % 4, pl.ds(skip, DOWN_ROWS - skip)]
        loads.append(pltpu.make_async_copy(piece, vmem[2].at[rows], local.at[2 + at]))
    for each in loads:
        each.start()
    return loads


def split_rows(value, parts):
    for index, (source, rows) in enumerate(parts):
        yield source, rows, value[64 * index : 64 * index + 64]


def mlp_forward_kernel(
    normed_ref, hidden_ref, gate_hbm, up_hbm, down_hbm, out_ref, all_ref, gate_ref, up_ref,
    gate_w, up_w, down_w, total_ref, near_terms, part, far_part, near_sum, part_in, far_in, near_in, send, recv, local
):
    loads = mlp_start((gate_hbm, up_hbm, down_hbm), (gate_w, up_w, down_w), local)

    def work(parts):
        rows = jnp.concatenate([all_ref[source, rows] for source, rows in parts], axis=0)
        gate = nn(rows, gate_w[...])
        up = nn(rows, up_w[...])
        for source, at, value in split_rows(gate, parts):
            gate_ref[source, at] = value.astype(BF)
        for source, at, value in split_rows(up, parts):
            up_ref[source, at] = value.astype(BF)
        product = (gate * jax.nn.sigmoid(gate) * up).astype(BF)
        return nn(product, down_w[...])

    total = exchange(
        normed_ref, all_ref, total_ref, near_terms, part, far_part, near_sum, part_in, far_in, near_in,
        Copies(send, recv), loads, work
    )
    out_ref[...] = (hidden_ref[...] + total).astype(BF)


def mlp_forward(normed2, hidden, gate_w, up_w, down_w):
    return pl.pallas_call(
        mlp_forward_kernel,
        out_shape=(
            shaped(ROWS, D),
            shaped(4, ROWS, D),
            shaped(4, ROWS, QUARTER),
            shaped(4, ROWS, QUARTER),
        ),
        in_specs=[VMEM_SPEC] * 2 + [ANY_SPEC] * 3,
        scratch_shapes=EXCHANGE_SCRATCH,
        compiler_params=params(3),
        name="mlp_forward",
    )(normed2, hidden, gate_w, up_w, down_w)


def mlp_backward_kernel(
    dout_ref, gate_ref, up_ref, gate_hbm, up_hbm, down_hbm,
    dnormed_ref, all_ref, dgate_ref, dup_ref, product_ref,
    gate_w, up_w, down_w, total_ref, near_terms, part, far_part, near_sum, part_in, far_in, near_in, send, recv, local
):
    loads = mlp_start((gate_hbm, up_hbm, down_hbm), (gate_w, up_w, down_w), local)

    def work(parts):

        def stacked(ref):
            return jnp.concatenate([ref[source, rows] for source, rows in parts], axis=0)

        dproduct = nt(stacked(all_ref), down_w[...])
        gate = stacked(gate_ref).astype(F32)
        up = stacked(up_ref).astype(F32)
        s = jax.nn.sigmoid(gate)
        silu = gate * s
        product = (silu * up).astype(BF)
        dgate = (dproduct * up * (s * (1.0 + gate * (1.0 - s)))).astype(BF)
        dup = (dproduct * silu).astype(BF)
        for to, whole in ((product_ref, product), (dgate_ref, dgate), (dup_ref, dup)):
            for source, at, value in split_rows(whole, parts):
                to[source, at] = value
        return nt(dgate, gate_w[...]) + nt(dup, up_w[...])

    dnormed_ref[...] = exchange(
        dout_ref, all_ref, total_ref, near_terms, part, far_part, near_sum, part_in, far_in, near_in,
        Copies(send, recv), loads, work
    )


def mlp_backward(dout, gate, up, gate_w, up_w, down_w):
    return pl.pallas_call(
        mlp_backward_kernel,
        out_shape=(
            shaped(ROWS, D, dtype=F32),
            shaped(4, ROWS, D),
            shaped(4, ROWS, QUARTER),
            shaped(4, ROWS, QUARTER),
            shaped(4, ROWS, QUARTER),
        ),
        in_specs=[VMEM_SPEC] * 3 + [ANY_SPEC] * 3,
        scratch_shapes=EXCHANGE_SCRATCH,
        compiler_params=params(4),
        name="mlp_backward",
    )(dout, gate, up, gate_w, up_w, down_w)


def outputs_kernel(
    gate, up, down, qkv, out, gate_out, up_out, down_out, qkv_out, out_out, bias_out, value_out, gain1_out, gain2_out
):
    for r in range(4):
        lanes = slice(QUARTER * r, QUARTER * r + QUARTER)
        gate_out[:, lanes] = gate[r].astype(F32)
        up_out[:, lanes] = up[r].astype(F32)
        skip = 80 * r - DOWN_STARTS[r]
        down_out[80 * r : DOWN_STARTS[r] + DOWN_ROWS] = down[r, skip:].astype(F32)
    qkv_out[:32] = qkv[0]
    qkv_out[32:] = qkv[1, :24]
    out_out[:32] = out[0]
    out_out[32:] = out[1, :24]
    small = qkv[1, 24:][:1]
    bias_out[...] = small[:, :64]
    value_out[...] = small[:, 64:72]
    gain1_out[...] = small[:, 72:128]
    gain2_out[...] = small[:, 128:184]


def outputs(gate, up, down, qkv, out):
    return local_call(
        outputs_kernel,
        "outputs",
        (
            shaped(56, FF, dtype=F32),
            shaped(56, FF, dtype=F32),
            shaped(FF // 16, D, dtype=F32),
            shaped(56, QKV, dtype=F32),
            shaped(56, D, dtype=F32),
            shaped(1, 64, dtype=F32),
            shaped(1, 8, dtype=F32),
            shaped(1, 56, dtype=F32),
            shaped(1, 56, dtype=F32),
        ),
    )(gate, up, down, qkv, out)


def turn(values, cosine, sine, sign):
    width = values.shape[1]
    up = pltpu.roll(values, width - HALF, 1)
    down = pltpu.roll(values, HALF, 1)
    lane = lax.broadcasted_iota(jnp.int32, values.shape, 1)
    swapped = jnp.where(lax.rem(lane, 2 * HALF) < HALF, up, down)
    repeat = width // KV
    cosine = jnp.concatenate([cosine] * repeat, axis=1)
    sine = jnp.concatenate([sine] * repeat, axis=1)
    return values * cosine + sign * (swapped * sine)


def front_work(x_ref, w_ref, b_ref, g_ref, cos_ref, sin_ref, normed_ref, q_ref, kv_ref, copies, ready):
    z, y, along_y, along_z = grid_place()
    x = x_ref[...].astype(F32)
    inverse = lax.rsqrt(jnp.mean(x * x, axis=-1, keepdims=True) + EPSILON)
    normed = (x * inverse * g_ref[...]).astype(BF)
    normed_ref[...] = normed
    projected = nn(normed, w_ref[:, D:]) + b_ref[:, D:]
    turned = turn(projected[:, :KV], cos_ref[...], sin_ref[...], 1.0)
    kv = jnp.concatenate([turned, projected[:, KV:]], axis=1).astype(BF)
    kv_ref[0, z, y] = kv[:64]
    kv_ref[1, z, y] = kv[64:]
    if ready:
        ready()
    top, bottom = (slice(0, 32), slice(None)), (slice(32, 64), slice(None))
    steps = gather_both(
        y_then_z(kv_ref.at[0], *top),
        y_then_z(kv_ref.at[0], *bottom),
        z_then_y(kv_ref.at[1], *top),
        z_then_y(kv_ref.at[1], *bottom),
        copies,
    )
    next(steps)
    projected = nn(normed, w_ref[:, :D]) + b_ref[:, :D]
    q_ref[...] = turn(projected, cos_ref[...], sin_ref[...], 1.0).astype(BF)
    return steps


def front_kernel(x_ref, w_ref, b_ref, g_ref, cos_ref, sin_ref, normed_ref, q_ref, kv_ref, send, recv):
    z, y, along_y, along_z = grid_place()
    signal(neighbours(along_y, along_z))
    steps = front_work(
        x_ref, w_ref, b_ref, g_ref, cos_ref, sin_ref, normed_ref, q_ref, kv_ref,
        Copies(send, recv), lambda: greeted(4)
    )
    run(steps)


def front(x, w_qkv, b_qkv, g_attn, cosine, sine):
    return pl.pallas_call(
        front_kernel,
        out_shape=(shaped(ROWS, D), shaped(ROWS, D), shaped(2, 4, 4, 64, 2 * KV)),
        scratch_shapes=[pltpu.SemaphoreType.DMA((24,)), pltpu.SemaphoreType.DMA((24,))],
        compiler_params=params(6),
        name="front",
    )(x, w_qkv, b_qkv, g_attn, cosine, sine)


def low_lanes(rows):
    return lax.broadcasted_iota(jnp.int32, (rows, KV), 1) < KV // 2


def spread(kv_ref, start, to_ref):
    mixed = kv_ref[:, :, :, :, start : start + KV].reshape(LEN, KV)
    other = pltpu.roll(mixed.astype(F32), KV // 2, 1).astype(BF)
    low = low_lanes(LEN)
    to_ref[0] = jnp.where(low, mixed, other)
    to_ref[1] = mixed
    to_ref[2] = jnp.where(low, other, mixed)


def fill_bias(kseg_ref, bias_refs):
    first_row = 64 * lax.axis_index("group")
    for block, bias_ref in enumerate(bias_refs):
        keys = SPAN * (block + 1)
        kpos = lax.broadcasted_iota(jnp.int32, (64, keys), 1)
        qpos = SPAN * block + first_row + lax.broadcasted_iota(jnp.int32, (64, keys), 0)
        kseg = jnp.broadcast_to(kseg_ref[:, :keys], (64, keys)).astype(F32)
        qseg = jnp.sum(jnp.where(kpos == qpos, kseg, 0.0), axis=1, keepdims=True)
        bias_ref[...] = jnp.where((kpos <= qpos) & (kseg == qseg), 0.0, NEGATIVE)


def two_heads(pair):
    low = low_lanes(64)
    zero = jnp.zeros_like(pair)
    return jnp.concatenate([jnp.where(low, pair, zero), jnp.where(low, zero, pair)], axis=0)


def one_pair(stacked):
    return jnp.where(low_lanes(64), stacked[:64], stacked[64:])


def softmax(queries, keys, bias_ref):
    count = keys.shape[0]
    scores = nt(queries, keys).reshape(2, 64, count) + bias_ref[...][None]
    highest = jnp.max(scores, axis=-1, keepdims=True)
    exponent = jnp.exp(scores - highest)
    total = jnp.sum(exponent, axis=-1, keepdims=True)
    return (exponent * (1.0 / total)).reshape(2 * 64, count)


def variant_of(pair):
    return jnp.where(pair < 3, 0, jnp.where(pair == 3, 1, 2))


def attention_work(
    x_ref, q_ref, kv_ref, kseg_ref, w_ref, g_ref, context_ref, hidden_ref, normed_ref,
    keys_ref, values_ref, bias0, bias1, between=None
):
    spread(kv_ref, 0, keys_ref)
    spread(kv_ref, KV, values_ref)
    fill_bias(kseg_ref, (bias0, bias1))

    def one(pair, carry):
        if between:
            pl.when(pair == 4)(between)
        variant = variant_of(pair)
        lanes = pl.ds(pl.multiple_of(pair * KV, KV), KV)
        for block, bias_ref in enumerate((bias0, bias1)):
            rows = slice(64 * block, 64 * block + 64)
            keys = pl.ds(0, SPAN * (block + 1))
            queries = two_heads(q_ref[rows, lanes] * SCALE).astype(BF)
            weights = softmax(queries, keys_ref[variant, keys], bias_ref).astype(BF)
            context = nn(weights, values_ref[variant, keys])
            context_ref[rows, lanes] = one_pair(context).astype(BF)
        return carry

    lax.fori_loop(0, PAIRS, one, 0)
    hidden = x_ref[...].astype(F32) + nn(context_ref[...], w_ref[...])
    hidden_ref[...] = hidden
    inverse = lax.rsqrt(jnp.mean(hidden * hidden, axis=-1, keepdims=True) + EPSILON)
    normed_ref[...] = (hidden * inverse * g_ref[...]).astype(BF)


ATTENTION_SCRATCH = [
    pltpu.VMEM((3, LEN, KV), BF),
    pltpu.VMEM((3, LEN, KV), BF),
    pltpu.VMEM((64, SPAN), F32),
    pltpu.VMEM((64, LEN), F32),
]


def attention(x, q, kv, kseg, w_out, g_mlp):
    return local_call(
        attention_work,
        "attention",
        (shaped(ROWS, D), shaped(ROWS, D, dtype=F32), shaped(ROWS, D)),
        ATTENTION_SCRATCH,
    )(x, q, kv, kseg, w_out, g_mlp)


def norm_backward(values, gain, grads):
    inverse = lax.rsqrt(jnp.mean(values * values, axis=-1, keepdims=True) + EPSILON)
    scaled = grads * gain
    dvalues = inverse * scaled - values * (
        inverse * inverse * inverse * jnp.mean(scaled * values, axis=-1, keepdims=True)
    )
    return dvalues, jnp.sum(grads * values * inverse, axis=0, keepdims=True)


def attention_backward_work(
    dout_ref, dnormed_ref, hidden_ref, g_ref, w_ref, q_ref, kv_ref, kseg_ref,
    dhidden_ref, dlow_ref, dq_ref, dkv_ref, dgain_ref,
    keys_ref, values_ref, bias0, bias1, dcontext_ref, dkeys, dvalues, between=None
):
    dnorm, dgain = norm_backward(hidden_ref[...], g_ref[...], dnormed_ref[...])
    dgain_ref[...] = dgain
    dhidden = dout_ref[...].astype(F32) + dnorm
    dhidden_ref[...] = dhidden
    dlow = dhidden.astype(BF)
    dlow_ref[...] = dlow
    dcontext_ref[...] = nt(dlow, w_ref[...]).astype(BF)
    spread(kv_ref, 0, keys_ref)
    spread(kv_ref, KV, values_ref)
    fill_bias(kseg_ref, (bias0, bias1))
    dkeys[...] = jnp.zeros_like(dkeys)
    dvalues[...] = jnp.zeros_like(dvalues)

    def one(pair, carry):
        if between:
            pl.when(pair == 4)(between)
        variant = variant_of(pair)
        lanes = pl.ds(pl.multiple_of(pair * KV, KV), KV)
        for block, bias_ref in enumerate((bias0, bias1)):
            rows = slice(64 * block, 64 * block + 64)
            keys = pl.ds(0, SPAN * (block + 1))
            queries = two_heads(q_ref[rows, lanes] * SCALE).astype(BF)
            dcontext = two_heads(dcontext_ref[rows, lanes])
            key_rows = keys_ref[variant, keys]
            weights = softmax(queries, key_rows, bias_ref)
            dweights = nt(dcontext, values_ref[variant, keys])
            inner = jnp.sum(weights * dweights, axis=-1, keepdims=True)
            dscores = (weights * (dweights - inner)).astype(BF)
            dq_ref[rows, lanes] = one_pair(nn(dscores, key_rows)) * SCALE
            dkeys[variant, keys] += tn(dscores, queries)
            dvalues[variant, keys] += tn(weights.astype(BF), dcontext)
        return carry

    lax.fori_loop(0, PAIRS, one, 0)
    low = low_lanes(LEN)
    for start, total in ((0, dkeys), (KV, dvalues)):
        head0 = total[0] + pltpu.roll(total[0], KV // 2, 1)
        head1 = total[2] + pltpu.roll(total[2], KV // 2, 1)
        whole = (jnp.where(low, head0, head1) + total[1]).astype(BF)
        dkv_ref[:, :, :, :, start : start + KV] = whole.reshape(2, 4, 4, 64, KV)


ATTENTION_BACKWARD_OUT = (
    shaped(ROWS, D, dtype=F32),
    shaped(ROWS, D),
    shaped(ROWS, D, dtype=F32),
    shaped(2, 4, 4, 64, 2 * KV),
    shaped(1, D, dtype=F32),
)
ATTENTION_BACKWARD_SCRATCH = ATTENTION_SCRATCH + [
    pltpu.VMEM((ROWS, D), BF),
    pltpu.VMEM((3, LEN, KV), F32),
    pltpu.VMEM((3, LEN, KV), F32),
]


def attention_backward(*operands):
    return local_call(
        attention_backward_work, "attention_backward", ATTENTION_BACKWARD_OUT, ATTENTION_BACKWARD_SCRATCH
    )(*operands)


def rear_query(dq_ref, cos_ref, sin_ref, w_ref, dprojected_ref, dbias_ref):
    dquery = turn(dq_ref[...], cos_ref[...], sin_ref[...], -1.0).astype(BF)
    dprojected_ref[:, :D] = dquery
    dbias_ref[:, :D] = jnp.sum(dquery.astype(F32), axis=0, keepdims=True)
    return nt(dquery, w_ref[:, :D])


def rear_rest(
    dnormed, total, cos_ref, sin_ref, w_ref, x_ref, g_ref, dhidden_ref, dprojected_ref, dinput_ref, dgain_ref, dbias_ref
):
    turned = turn(total[:, :KV], cos_ref[...], sin_ref[...], -1.0)
    dkv = jnp.concatenate([turned, total[:, KV:]], axis=1).astype(BF)
    dprojected_ref[:, D:] = dkv
    dbias_ref[:, D:] = jnp.sum(dkv.astype(F32), axis=0, keepdims=True)
    dnormed = dnormed + nt(dkv, w_ref[:, D:])
    dnorm, dgain = norm_backward(x_ref[...].astype(F32), g_ref[...], dnormed)
    dgain_ref[...] = dgain
    dinput_ref[...] = (dhidden_ref[...] + dnorm).astype(BF)


REAR_SCRATCH = [
    pltpu.VMEM((ROWS, QKV), BF),
    pltpu.VMEM((1, D), F32),
    pltpu.VMEM((1, QKV), F32),
    pltpu.VMEM((ROWS, 2 * KV), F32),
] + scatter_scratch(*[(32, 2 * KV)] * 4)


def rear_kernel(
    dkv_ref, dq_ref, cos_ref, sin_ref, w_ref, x_ref, g_ref, dhidden_ref, dinput_ref,
    dprojected_ref, dgain_ref, dbias_ref, total, *rest
):
    scratch, (send, recv) = rest[:-2], rest[-2:]
    z, y, along_y, along_z = grid_place()
    signal(neighbours(along_y, along_z))
    greeted(4)
    steps = kv_sums(dkv_ref, total, scratch, Copies(send, recv))
    next(steps)
    dnormed = rear_query(dq_ref, cos_ref, sin_ref, w_ref, dprojected_ref, dbias_ref)
    run(steps)
    rear_rest(
        dnormed, total, cos_ref, sin_ref, w_ref, x_ref, g_ref, dhidden_ref,
        dprojected_ref, dinput_ref, dgain_ref, dbias_ref
    )


def rear(dkv, dq, cosine, sine, w_qkv, x, g_attn, dhidden):
    return pl.pallas_call(
        rear_kernel,
        out_shape=shaped(ROWS, D),
        scratch_shapes=REAR_SCRATCH + [pltpu.SemaphoreType.DMA((24,)), pltpu.SemaphoreType.DMA((24,))],
        compiler_params=params(7),
        name="rear",
    )(dkv, dq, cosine, sine, w_qkv, x, g_attn, dhidden)


TAIL_SCRATCH = [
    pltpu.VMEM((4, 4, 56, QUARTER), BF),
    pltpu.VMEM((4, 4, 56, QUARTER), BF),
    pltpu.VMEM((4, 4, DOWN_ROWS, D), BF),
    pltpu.VMEM((56, QUARTER), BF),
    pltpu.VMEM((56, QUARTER), BF),
    pltpu.VMEM((DOWN_ROWS, D), BF),
    pltpu.VMEM((4, 4, 64, QKV), BF),
    pltpu.VMEM((4, 4, 64, D), BF),
    pltpu.VMEM((4, 4, 32, QKV), BF),
    pltpu.VMEM((4, 4, 32, D), BF),
    pltpu.VMEM((32, QKV), F32),
    pltpu.VMEM((32, D), F32),
    pltpu.VMEM((32, QKV), BF),
    pltpu.VMEM((32, D), BF),
    pltpu.VMEM((32, QKV), BF),
    pltpu.VMEM((32, D), BF),
]
TAIL_COPIES = 24 + 36 + 24 + 2 + 13


def tail_kernel(*refs):
    refs = list(refs)

    def take(count):
        taken = refs[:count]
        del refs[:count]
        return taken

    attention_in = take(8)
    mlp_in = take(5)
    cos_ref, sin_ref, qkv_w, x_ref, gain1_ref, normed_ref, context_ref = take(7)
    dinput_ref, gate_all, up_all, down_all, qkv_all, out_all = take(6)
    attention_out = take(5)
    dhidden_ref, dlow_ref, dq_ref, dkv_ref, dgain2_ref = attention_out
    attention_scratch = take(len(ATTENTION_BACKWARD_SCRATCH))
    dprojected_ref, dgain1_ref, dbias_ref, total = take(4)
    kv_bufs = take(24)
    mlp_term_refs, mlp_sum_refs = take(3), take(3)
    qkv_terms, out_terms, qkv_half, out_half, qkv_sum, out_sum, qkv_low, out_low, qkv_in, out_in = take(10)
    mlp_bufs, qkv_bufs = take(24), take(24)
    send, recv, local = take(3)

    z, y, along_y, along_z = grid_place()
    me, mate, next_, far = replica_partners()
    core = lax.rem(me, 2)
    to_mate, to_next = {"replica": mate}, {"replica": next_}
    target, source, stays = quarter_route()
    moves = jnp.logical_not(stays)
    signal(neighbours(along_y, along_z) + [to_mate, to_next])
    mlp_terms(*mlp_in, *mlp_term_refs)

    @pl.when(moves)
    def _():
        signal([target])
        greeted(7)

    @pl.when(stays)
    def _():
        greeted(6)

    copies = Copies(send, recv)
    mlp = mlp_sums(*mlp_term_refs, *mlp_sum_refs, mlp_bufs, copies)
    next(mlp)
    attention_backward_work(*attention_in, *attention_out, *attention_scratch, lambda: next(mlp))
    kv = kv_sums(dkv_ref, total, kv_bufs, copies)
    next(kv)
    next(mlp)

    mine = pl.ds(pl.multiple_of(32 * core, 32), 32)
    theirs = pl.ds(pl.multiple_of(32 - 32 * core, 32), 32)

    def add_mate(sent, terms, half):
        sent.wait_recv()
        half[...] = (terms[:, :, mine].astype(F32) + half[...].astype(F32)).astype(BF)

    dnormed = rear_query(dq_ref, cos_ref, sin_ref, qkv_w, dprojected_ref, dbias_ref)
    next(kv)
    whole = tn(context_ref[...], dlow_ref[...])
    for at in range(16):
        rows = jnp.concatenate([whole[56 * at : 56 * at + 56], jnp.zeros((8, D), F32)], axis=0)
        out_terms[at // 4, at % 4] = rows.astype(BF)
    out_sent = copies(out_terms.at[:, :, theirs], out_half, to_mate)
    next(kv)
    add_mate(out_sent, out_terms, out_half)
    run(kv)
    rear_rest(
        dnormed, total, cos_ref, sin_ref, qkv_w, x_ref, gain1_ref, dhidden_ref,
        dprojected_ref, dinput_ref, dgain1_ref, dbias_ref
    )
    whole = tn(normed_ref[...], dprojected_ref[...])
    dbias, dgain1, dgain2 = dbias_ref[...], dgain1_ref[...], dgain2_ref[...]
    for at in range(16):
        small = jnp.concatenate(
            [
                dbias[:, 64 * at : 64 * at + 64],
                dbias[:, D + KV + 8 * at : D + KV + 8 * at + 8],
                dgain1[:, 56 * at : 56 * at + 56],
                dgain2[:, 56 * at : 56 * at + 56],
                jnp.zeros((1, QKV - 184), F32),
            ],
            axis=1,
        )
        rows = jnp.concatenate([whole[56 * at : 56 * at + 56], jnp.broadcast_to(small, (8, QKV))], axis=0)
        qkv_terms[at // 4, at % 4] = rows.astype(BF)
    qkv_sent = copies(qkv_terms.at[:, :, theirs], qkv_half, to_mate)
    next(mlp)
    add_mate(qkv_sent, qkv_terms, qkv_half)
    dense = qkv_sums(qkv_half, out_half, qkv_sum, out_sum, qkv_bufs, copies)
    next(dense)
    next(mlp)
    next(dense)
    run(mlp)

    gate, up, down = mlp_sum_refs
    moved = pltpu.make_async_remote_copy(
        src_ref=down,
        dst_ref=down_all.at[source["replica"]],
        send_sem=local.at[0],
        recv_sem=local.at[1],
        device_id=source,
        device_id_type=MESH,
    )
    stayed = pltpu.make_async_copy(down, down_all.at[me], local.at[2])

    @pl.when(moves)
    def _():
        moved.start()

    @pl.when(stays)
    def _():
        stayed.start()

    pairs = ((gate, gate_all), (up, up_all))
    across = [copies(ref, all_ref.at[me], to_next) for ref, all_ref in pairs]
    beside = [copies(ref, all_ref.at[me], to_mate) for ref, all_ref in pairs]
    for ref, all_ref in pairs:
        all_ref[me] = ref[...]
    next(dense)

    @pl.when(moves)
    def _():
        moved.wait()

    @pl.when(stays)
    def _():
        stayed.wait()

    across.append(copies(down_all.at[me], down_all.at[me], to_next))
    beside.append(copies(down_all.at[me], down_all.at[me], to_mate))
    next(dense)
    run(dense)
    qkv_low[...] = qkv_sum[...].astype(BF)
    out_low[...] = out_sum[...].astype(BF)
    sums = [copies(qkv_low, qkv_in, to_next), copies(out_low, out_in, to_next)]
    for came, all_ref in zip(across, (gate_all, up_all, down_all)):
        came.wait_recv()
        beside.append(copies(all_ref.at[next_], all_ref.at[next_], to_mate))
    sums[0].wait_recv()
    qkv_all[core] = qkv_sum[...] + qkv_in[...].astype(F32)
    sums[1].wait_recv()
    out_all[core] = out_sum[...] + out_in[...].astype(F32)
    beside += [copies(ref.at[core], ref.at[core], to_mate) for ref in (qkv_all, out_all)]
    for each in beside:
        each.wait_recv()
    for each in [out_sent, qkv_sent] + across + beside + sums:
        each.wait_send()


def tail(*operands):
    return pl.pallas_call(
        tail_kernel,
        out_shape=(
            shaped(ROWS, D),
            shaped(4, 56, QUARTER),
            shaped(4, 56, QUARTER),
            shaped(4, DOWN_ROWS, D),
            shaped(2, 32, QKV, dtype=F32),
            shaped(2, 32, D, dtype=F32),
        ),
        scratch_shapes=[pltpu.VMEM(each.shape, each.dtype) for each in ATTENTION_BACKWARD_OUT]
        + ATTENTION_BACKWARD_SCRATCH
        + REAR_SCRATCH
        + TAIL_SCRATCH
        + scatter_scratch(*MLP_SUMS_SHAPES)
        + scatter_scratch((16, QKV), (16, QKV), (16, D), (16, D))
        + [
            pltpu.SemaphoreType.DMA((TAIL_COPIES,)),
            pltpu.SemaphoreType.DMA((TAIL_COPIES,)),
            pltpu.SemaphoreType.DMA((3,)),
        ],
        compiler_params=params(1),
        name="tail",
    )(*operands)


def rotary(group):
    lane = np.arange(KV)
    frequency = jnp.asarray(THETA ** (-(lane % HALF) * 2.0 / (2 * HALF)), F32)
    sign = jnp.asarray(np.where(lane % (2 * HALF) < HALF, -1.0, 1.0), F32)
    row = lax.broadcasted_iota(jnp.int32, (ROWS, KV), 0)
    positions = group * 64 + lax.rem(row, 64) + SPAN * (row // 64)
    angles = positions.astype(F32) * frequency[None, :]
    return jnp.cos(angles), jnp.sin(angles) * sign[None, :]


def body(inputs, cotangent, segments, w_qkv, b_qkv, w_out, w_gate, w_up, w_down, g_attn, g_mlp):
    section = lax.axis_index("section")
    group = lax.axis_index("group")
    replica = lax.axis_index("replica")
    core = lax.rem(replica, 2)

    down_piece = lax.dynamic_slice(w_down[0], (jnp.minimum(80 * replica, 224), 0), (DOWN_ROWS, D))
    gate_piece = lax.dynamic_slice(w_gate[0], (0, replica * QUARTER), (D // 16, QUARTER))
    up_piece = lax.dynamic_slice(w_up[0], (0, replica * QUARTER), (D // 16, QUARTER))
    small = jnp.concatenate([b_qkv[0], g_attn[0], g_mlp[0]])
    small = jnp.pad(small[None], ((0, 7), (0, QKV - small.shape[0])))
    qkv_piece = lax.dynamic_slice(jnp.concatenate([w_qkv[0], small], axis=0), (32 * core, 0), (32, QKV))
    out_piece = lax.dynamic_slice(jnp.pad(w_out[0], ((0, 8), (0, 0))), (32 * core, 0), (32, D))

    cosine, sine = rotary(group)
    kseg = segments
    x_in = inputs[0].reshape(ROWS, D)
    cotangent_in = cotangent[0].reshape(ROWS, D)
    gate_w, up_w, down_w, qkv_w, out_w, bias, gain1, gain2, hidden, normed2 = first(
        gate_piece, up_piece, down_piece, qkv_piece, out_piece, x_in, cosine, sine, kseg
    )
    gate_w = gate_w.reshape(D, QUARTER)
    up_w = up_w.reshape(D, QUARTER)

    def forward(x):
        normed, q, kv = front(x, qkv_w, bias, gain1, cosine, sine)
        context, hidden, normed2 = attention(x, q, kv, kseg, out_w, gain2)
        output, normed2_all, gate, up = mlp_forward(normed2, hidden, gate_w, up_w, down_w)
        return output, (x, normed, q, kv, context, hidden, normed2_all, gate, up)

    def backward_start(dout):
        dnormed2, *grads = mlp_backward(dout, gate, up, gate_w, up_w, down_w)
        dout_all, dgate, dup, product = grads
        return (dout, dnormed2, hidden, gain2, out_w, q, kv, kseg), (normed2_all, dgate, dup, product, dout_all)

    relayed, *_ = mlp_forward(normed2, hidden, gate_w, up_w, down_w)
    relayed = lax.ppermute(relayed, "section", [(0, 1)])
    output, kept = forward(jnp.where(section == 0, x_in, relayed))
    x, normed, q, kv, context, hidden, normed2_all, gate, up = kept
    operands, _ = backward_start(cotangent_in)
    dhidden, _, dq, dkv, _ = attention_backward(*operands)
    returned = rear(dkv, dq, cosine, sine, qkv_w, x, gain1, dhidden)
    returned = lax.ppermute(returned, "section", [(1, 0)])
    operands, mlp_operands = backward_start(jnp.where(section == 1, cotangent_in, returned))
    dinput, *parts = tail(*operands, *mlp_operands, cosine, sine, qkv_w, x, gain1, normed, context)
    grad_gate, grad_up, grad_down, grad_qkv, grad_out, bias, value_bias, gain1, gain2 = outputs(*parts)
    return (
        output.reshape(1, 1, 2, 64, D),
        dinput.reshape(1, 1, 2, 64, D),
        grad_qkv[None],
        bias,
        value_bias,
        grad_out[None],
        grad_gate[None],
        grad_up[None],
        grad_down[None],
        gain1,
        gain2,
    )


def solution(mesh):
    in_specs = (
        P("replica", None, "group", None),
        P("replica", None, "group", None),
        P("replica", None),
        P("section", "group", None),
        P("section", "group"),
        P("section", "group", None),
        P("section", "group", None),
        P("section", "group", None),
        P("section", "group", None),
        P("section", "group"),
        P("section", "group"),
    )
    out_specs = (
        P("section", "replica", None, "group", None),
        P("section", "replica", None, "group", None),
        P("section", "group", None),
        P("section", "group"),
        P("section", "group"),
        P("section", "group", None),
        P("section", "group", None),
        P("section", "group", None),
        P("section", "group", None),
        P("section", "group"),
        P("section", "group"),
    )
    return jax.shard_map(body, mesh=mesh, in_specs=in_specs, out_specs=out_specs, check_vma=False)
```

profile of v0, /device:TPU:1, one launch (start us, length us, event | category | flops | bytes accessed | tf_op | source)
XLA Modules:
  0.0 373.3 jit_solution(2027587296227153623)
XLA Ops:
  0.6 0.0 copy-start
  0.7 0.8 pad_maximum_fusion
  1.5 1.4 pad_dynamic-slice_fusion.2.out
  3.0 1.5 fusion.1.qkv
  4.4 0.0 copy-done
  4.4 0.7 dynamic-slice_bitcast_fusion.down
  5.1 1.8 dynamic-slice_bitcast_fusion.1
  7.0 1.7 sine_multiply_fusion
  8.7 74.5 %first.1 = (bf16[4,4,56,1216]{3,2,1,0:T(8,128)(2,1)}, bf16[4,4,56,1216]{3,2,1,0:T(8,128)(2,1)}, bf16[4,4,80,896]{3,2,1,0:T(8,128)(2,1)}, bf16[896,1152]{1,0:T(8,...) custom-call(bf16[56,1216]{1,0:T(8,128)(2,1)} %get-tuple-element.104., ...), custom_call_target="tpu_custom_call" | custom-call | tf_op jit(solution)/shard_map/first/pallas_call | solution.py:328
  83.1 0.0 copy-start.2
  83.1 23.4 %mlp_forward.2 = (bf16[128,896]{1,0:T(8,128)(2,1)}, bf16[4,128,896]{2,1,0:T(8,128)(2,1)}, bf16[4,128,1216]{2,1,0:T(8,128)(2,1)}, bf16[4,128,1216]{2,1,0:T(8,128)(2,1)}) custom-call(bf16[128,896]{1,0:T(8,128)(2,1)} %get-tuple-element.56.normed_ref, f32[128,896]{1,0:T(8,128)} %get-tuple-element.57.hidden_ref, bf16[896,1216]{1,0:T(8,128)(2,1)} %bitcast.24, ...), custom_call_target="tpu_custom_call" | custom-call | tf_op jit(solution)/shard_map/mlp_forward/pallas_call | solution.py:708
  106.6 5.2 %collective-permute-start = (bf16[128,896]{1,0:T(8,128)(2,1)}, bf16[128,896]{1,0:T(8,128)(2,1)S(1)}, u32[]{:S(2)}, u32[]{:S(2)}) collective-permute-start(bf16[128,896]{1,0:T(8,128)(2,1)} %get-tuple-element.61), channel_id=1, source_target_pairs={{0,64},{1,65},{2,66},{3,67},{4,68},{5,69},{6,70},{7,71},{8,72},{9,... | collective-permute-start | bytes 688136 | tf_op jit(solution)/shard_map/ppermute | solution.py:1335
  111.8 5.1 %collective-permute-done = bf16[128,896]{1,0:T(8,128)(2,1)S(1)} collective-permute-done((bf16[128,896]{1,0:T(8,128)(2,1)}, bf16[128,896]{1,0:T(8,128)(2,1)S(1)}, u32[]{:S(2)}, u32[]{:S(2)}) %collective-permute-start) | collective-permute-done | bytes 229408 | tf_op jit(solution)/shard_map/ppermute | solution.py:1335
  116.9 0.0 copy-done.2
  116.9 0.7 broadcast_select_fusion.1.x_ref.refs_16_
  117.7 16.1 %front.1 = (bf16[128,896]{1,0:T(8,128)(2,1)}, bf16[128,896]{1,0:T(8,128)(2,1)}, bf16[2,4,4,64,256]{4,3,2,1,0:T(8,128)(2,1)}) custom-call(bf16[128,896]{1,0:T(8,128)(2,1)} %broadcast_select_fusion.1.x_ref.refs_16_, bf16[896,1152]{1,0:T(8,128)(2,1)} %get-tuple-element.62.w_ref.refs_15_, f32[1,1152]{1,0:T(1,128)} %get-tuple-element.63.b_ref, ...), custom_call_target="tpu_custom_call" | custom-call | tf_op jit(solution)/shard_map/front/pallas_call | solution.py:859
  133.8 13.5 %attention.1 = (bf16[128,896]{1,0:T(8,128)(2,1)}, f32[128,896]{1,0:T(8,128)}, bf16[128,896]{1,0:T(8,128)(2,1)}) custom-call(bf16[128,896]{1,0:T(8,128)(2,1)} %broadcast_select_fusion.1.x_ref.refs_16_, bf16[128,896]{1,0:T(8,128)(2,1)} %get-tuple-element.65.q_ref.refs_5_, bf16[2,4,4,64,256]{4,3,2,1,0:T(8,128)(2,1)} %get-tuple-element.66.kv_ref.refs_6_, ...), custom_call_target="tpu_custom_call" | custom-call | tf_op jit(solution)/shard_map/attention/pallas_call | solution.py:953
  147.4 22.6 %mlp_forward.3 = (bf16[128,896]{1,0:T(8,128)(2,1)}, bf16[4,128,896]{2,1,0:T(8,128)(2,1)}, bf16[4,128,1216]{2,1,0:T(8,128)(2,1)}, bf16[4,128,1216]{2,1,0:T(8,128)(2,1)}) custom-call(bf16[128,896]{1,0:T(8,128)(2,1)} %get-tuple-element.69.normed_ref, f32[128,896]{1,0:T(8,128)} %get-tuple-element.70.hidden_ref.refs_2_, bf16[896,1216]{1,0:T(8,128)(2,1)} %bitcast.25, ...), custom_call_target="tpu_custom_call" | custom-call | tf_op jit(solution)/shard_map/mlp_forward/pallas_call | solution.py:708
  170.0 22.5 %mlp_backward.2 = (f32[128,896]{1,0:T(8,128)}, bf16[4,128,896]{2,1,0:T(8,128)(2,1)}, bf16[4,128,1216]{2,1,0:T(8,128)(2,1)}, bf16[4,128,1216]{2,1,0:T(8,128)(2,1)}, bf16[4,128,1216]{2,1,0:T(8,128)(2,1)}) custom-call(bf16[128,896]{1,0:T(8,128)(2,1)} %bitcast.32, bf16[4,128,1216]{2,1,0:T(8,128)(2,1)} %get-tuple-element.72.gate_ref, ...), custom_call_target="tpu_custom_call" | custom-call | tf_op jit(solution)/shard_map/mlp_backward/pallas_call | solution.py:755
  192.6 19.9 %attention_backward.1 = (f32[128,896]{1,0:T(8,128)}, bf16[128,896]{1,0:T(8,128)(2,1)}, f32[128,896]{1,0:T(8,128)}, bf16[2,4,4,64,256]{4,3,2,1,0:T(8,128)(2,1)}, f32[1,896]{1,0:T(1,128)}) custom-call(bf16[128,896]{1,0:T(8,128)(2,1)} %bitcast.33, f32[128,896]{1,0:T(8,128)} %get-tuple-element.74.dnormed_ref, f32[128,896]{1,0:T(8,128)} %get-tuple-element.70.hidden_ref.refs_2_, ...), custom_call_target="tpu_custom_call" | custom-call | tf_op jit(solution)/shard_map/attention_backward/pallas_call | solution.py:1032
  212.5 0.0 copy-start.1
  212.5 17.2 %rear.1 = bf16[128,896]{1,0:T(8,128)(2,1)} custom-call(bf16[2,4,4,64,256]{4,3,2,1,0:T(8,128)(2,1)} %get-tuple-element.75.dkv_ref, f32[128,896]{1,0:T(8,128)} %get-tuple-element.76.dq_ref, f32[128,128]{1,0:T(8,128)} %get-tuple-element.102.cos_ref.refs_13_, f32[128,128]{1,0:T(8,128)} %get-tuple-element.101.sin_ref.refs_14_, ...), custom_call_target="tpu_custom_call" | custom-call | tf_op jit(solution)/shard_map/rear/pallas_call | solution.py:1084
  229.7 1.3 collective-permute-start.1
  231.0 7.7 %collective-permute-done.1 = bf16[128,896]{1,0:T(8,128)(2,1)S(1)} collective-permute-done((bf16[128,896]{1,0:T(8,128)(2,1)}, bf16[128,896]{1,0:T(8,128)(2,1)S(1)}, u32[]{:S(2)}, u32[]{:S(2)}) %collective-permute-start.1) | collective-permute-done | bytes 229408 | tf_op jit(solution)/shard_map/ppermute | solution.py:1341
  238.7 0.0 copy-done.1
  238.7 0.7 broadcast_select_fusion.dout_ref.refs_0_
  239.5 26.9 %mlp_backward.3 = (f32[128,896]{1,0:T(8,128)}, bf16[4,128,896]{2,1,0:T(8,128)(2,1)}, bf16[4,128,1216]{2,1,0:T(8,128)(2,1)}, bf16[4,128,1216]{2,1,0:T(8,128)(2,1)}, bf16[4,128,1216]{2,1,0:T(8,128)(2,1)}) custom-call(bf16[128,896]{1,0:T(8,128)(2,1)} %broadcast_select_fusion.dout_ref.refs_0_, bf16[4,128,1216]{2,1,0:T(8,128)(2,1)} %get-tuple-element.72.gate_ref, ...), custom_call_target="tpu_custom_call" | custom-call | tf_op jit(solution)/shard_map/mlp_backward/pallas_call | solution.py:755
  266.4 101.4 %tail.1 = (bf16[128,896]{1,0:T(8,128)(2,1)}, bf16[4,56,1216]{2,1,0:T(8,128)(2,1)}, bf16[4,56,1216]{2,1,0:T(8,128)(2,1)}, bf16[4,80,896]{2,1,0:T(8,128)(2,1)}, f3...) custom-call(bf16[128,896]{1,0:T(8,128)(2,1)} %broadcast_select_fusion.dout_ref.refs_0_, ...), custom_call_target="tpu_custom_call" | custom-call | tf_op jit(solution)/shard_map/tail/pallas_call | solution.py:1263
  367.8 0.0 copy-start.3
  367.8 0.0 copy-start.4
  367.8 3.7 outputs.1
  371.5 0.0 copy-done.3
  371.5 0.7 copy.26
  372.2 0.0 copy-done.4
  372.2 0.7 copy.27
  (4 shorter events, 0.0 us)
Async XLA Ops:
  0.6 3.8 %copy-start = (bf16[1,304,896]{2,1,0:T(8,128)(2,1)S(1)}, bf16[1,304,896]{2,1,0:T(8,128)(2,1)}, u32[]{:S(2)}) copy-start(bf16[1,304,896]{2,1,0:T(8,128)(2,1)} %param.21) | copy-start | bytes 1634308
  83.1 33.8 %copy-start.2 = (bf16[1,2,64,896]{3,2,1,0:T(8,128)(2,1)S(1)}, bf16[1,2,64,896]{3,2,1,0:T(8,128)(2,1)}, u32[]{:S(2)}) copy-start(bf16[1,2,64,896]{3,2,1,0:T(8,128)(2,1)} %param.13) | copy-start | bytes 688132
  106.6 10.4 %collective-permute-start = (bf16[128,896]{1,0:T(8,128)(2,1)}, bf16[128,896]{1,0:T(8,128)(2,1)S(1)}, u32[]{:S(2)}, u32[]{:S(2)}) collective-permute-start(bf16[128,896]{1,0:T(8,128)(2,1)} %get-tuple-element.61), channel_id=1, source_target_pairs={{0,64},{1,65},{2,66},{3,67},{4,68},{5,69},{6,70},{7,71},{8,72},{9,... | collective-permute-start | bytes 688136 | tf_op jit(solution)/shard_map/ppermute | solution.py:1335
  212.5 26.2 %copy-start.1 = (bf16[1,2,64,896]{3,2,1,0:T(8,128)(2,1)S(1)}, bf16[1,2,64,896]{3,2,1,0:T(8,128)(2,1)}, u32[]{:S(2)}) copy-start(bf16[1,2,64,896]{3,2,1,0:T(8,128)(2,1)} %param.14) | copy-start | bytes 688132
  229.7 9.0 %collective-permute-start.1 = (bf16[128,896]{1,0:T(8,128)(2,1)}, bf16[128,896]{1,0:T(8,128)(2,1)S(1)}, u32[]{:S(2)}, u32[]{:S(2)}) collective-permute-start(bf16[128,896]{1,0:T(8,128)(2,1)} %rear.1), channel_id=1, source_target_pairs={{64,0},{65,1},{66,2},{67,3},{68,4},{69,5},{70,6},{71,7},{72,8},{73... | collective-permute-start | bytes 688136 | tf_op jit(solution)/shard_map/ppermute | solution.py:1341
  367.8 3.7 copy-start.3
  367.8 4.4 %copy-start.4 = (bf16[128,896]{1,0:T(8,128)(2,1)S(1)}, bf16[128,896]{1,0:T(8,128)(2,1)}, u32[]{:S(2)}) copy-start(bf16[128,896]{1,0:T(8,128)(2,1)} %get-tuple-element.86) | copy-start | bytes 688132
where the time goes:
time: 381 us; the launch traced here: 373 us
  Pallas kernels  342 us (90%)
  waiting for transfers between devices  12.9 us (3%)
  starting transfers between devices  6.5 us (2%)
  other arithmetic  5.5 us (1%)
  local copies, waits for them, and re-layouts  5.38 us (1%)
    pallas_call x1, Pallas kernels, tail(): pl.pallas_call(tail_kernel, out_shape=(shaped(ROWS, D), shaped(4, 56, QUA...  101 us
    pallas_call x1, Pallas kernels, first(): pl.pallas_call(first_kernel, out_shape=(shaped(4, 4, *gate.shape), shaped...  74.5 us
    pallas_call x2, Pallas kernels, mlp_backward(): pl.pallas_call(mlp_backward_kernel, out_shape=(shaped(ROWS, D, dtype=F32)...  49.5 us
    pallas_call x2, Pallas kernels, mlp_forward(): pl.pallas_call(mlp_forward_kernel, out_shape=(shaped(ROWS, D), shaped(4,...  46.1 us
    pallas_call x1, Pallas kernels, attention_backward(): local_call(attention_backward_work, 'attention_backward', ATTENTION_BACKW...  19.9 us
    pallas_call x1, Pallas kernels, rear(): pl.pallas_call(rear_kernel, out_shape=shaped(ROWS, D), scratch_shapes=REA...  17.2 us
    pallas_call x1, Pallas kernels, front(): pl.pallas_call(front_kernel, out_shape=(shaped(ROWS, D), shaped(ROWS, D),...  16.1 us
    pallas_call x1, Pallas kernels, attention(): local_call(attention_work, 'attention', (shaped(ROWS, D), shaped(ROWS, D,...  13.5 us
  transfers between devices with their start and end apart: 2, of which 2 were waited for; matrix products, arithmetic and copies ran while one was open for 0% of the time, Pallas kernels for 0%

commit v1 on v0

--- a/solution.py
+++ b/solution.py
@@ -90,7 +90,7 @@
 
 
 def neighbours(along_y, along_z):
-    return [along_y(1), along_y(3), along_z(1), along_z(3)]
+    return [along(step) for along in (along_y, along_z) for step in (1, 3, 2)]
 
 
 class Copies:
@@ -141,12 +141,30 @@
     return start, relay, finish
 
 
-def gather_both(first_a, second_a, first_b, second_b, copies):
+def gather_direct(firsts, seconds, place, device_at, copies):
+    sent = []
+    for block in firsts + seconds:
+        sent += [copies(block(place), block(place), device_at(step), False) for step in (1, 3, 2)]
+
+    def start():
+        for each in sent:
+            each.start()
+
+    def finish():
+        for each in sent:
+            each.wait_recv()
+        for each in sent:
+            each.wait_send()
+
+    return start, lambda: None, finish
+
+
+def gather_both(first_a, second_a, first_b, second_b, copies, phase=gather_phase):
     z, y, along_y, along_z = grid_place()
-    start_a, relay_a, finish_a = gather_phase([first_a[0]], [second_a[0]], y, along_y, copies)
-    start_b, relay_b, finish_b = gather_phase([first_b[0]], [second_b[0]], z, along_z, copies)
-    then_a, last_a, end_a = gather_phase([first_a[1]], [second_a[1]], z, along_z, copies)
-    then_b, last_b, end_b = gather_phase([first_b[1]], [second_b[1]], y, along_y, copies)
+    start_a, relay_a, finish_a = phase([first_a[0]], [second_a[0]], y, along_y, copies)
+    start_b, relay_b, finish_b = phase([first_b[0]], [second_b[0]], z, along_z, copies)
+    then_a, last_a, end_a = phase([first_a[1]], [second_a[1]], z, along_z, copies)
+    then_b, last_b, end_b = phase([first_b[1]], [second_b[1]], y, along_y, copies)
     start_a()
     start_b()
     yield
@@ -255,12 +273,12 @@
     @pl.when(moves)
     def _():
         signal([source])
-        greeted(6)
+        greeted(8)
         moved.start()
 
     @pl.when(stays)
     def _():
-        greeted(5)
+        greeted(7)
         stayed.start()
 
     copies = Copies(send, recv)
@@ -402,7 +420,35 @@
     return start, pass_on, finish
 
 
-def scatter_both(first_a, second_a, first_b, second_b, copies):
+def scatter_direct(firsts, seconds, place, device_at, copies):
+    parts = firsts + seconds
+    sent = []
+    for block, bufs, put in parts:
+        sent.append(
+            [
+                copies(block(lax.rem(place + step, 4)), bufs[index], device_at(step), False)
+                for index, step in enumerate((1, 3, 2))
+            ]
+        )
+
+    def start():
+        for each in sum(sent, []):
+            each.start()
+
+    def finish():
+        for came, (block, bufs, put) in zip(sent, parts):
+            total = block(place)[...].astype(F32)
+            for each, landed in zip(came, bufs):
+                each.wait_recv()
+                total = total + landed[...].astype(F32)
+            for each in came:
+                each.wait_send()
+            put(total)
+
+    return start, lambda: None, finish
+
+
+def scatter_both(first_a, second_a, first_b, second_b, copies, phase=scatter_phase):
     z, y, along_y, along_z = grid_place()
 
     def wide(part):
@@ -413,10 +459,10 @@
         _, kept, bufs, put = part
         return [((lambda at: kept[1].at[at]), bufs, put)]
 
-    start_a, pass_a, finish_a = scatter_phase(wide(first_a), wide(second_a), y, along_y, copies)
-    start_b, pass_b, finish_b = scatter_phase(wide(first_b), wide(second_b), z, along_z, copies)
-    then_a, last_a, end_a = scatter_phase(slim(first_a), slim(second_a), z, along_z, copies)
-    then_b, last_b, end_b = scatter_phase(slim(first_b), slim(second_b), y, along_y, copies)
+    start_a, pass_a, finish_a = phase(wide(first_a), wide(second_a), y, along_y, copies)
+    start_b, pass_b, finish_b = phase(wide(first_b), wide(second_b), z, along_z, copies)
+    then_a, last_a, end_a = phase(slim(first_a), slim(second_a), z, along_z, copies)
+    then_b, last_b, end_b = phase(slim(first_b), slim(second_b), y, along_y, copies)
     start_a()
     start_b()
     yield
@@ -557,6 +603,7 @@
         scatter_part(scratch, 2, lambda at: dkv_ref.at[1, at, :, top], stored_in(total, slice(64, 96))),
         scatter_part(scratch, 3, lambda at: dkv_ref.at[1, at, :, bottom], stored_in(total, slice(96, 128))),
         copies,
+        scatter_direct,
     )
 
 
@@ -565,13 +612,17 @@
     return me, me + 1 - 2 * lax.rem(me, 2), lax.rem(me + 2, 4), 3 - me
 
 
+def other_section():
+    return {"section": 1 - lax.axis_index("section")}
+
+
 def exchange(
-    own_ref, all_ref, total_ref, near_terms, part, far_part, near_sum, part_in, far_in, near_in, copies, loads, work
+    own_ref, all_ref, total_ref, near_terms, part, far_part, near_sum, part_in, far_in, near_in, copies, loads, work, greetings=2
 ):
     me, mate, next_, far = replica_partners()
     halves = (slice(0, 64), slice(64, 128))
     to_mate, to_next = {"replica": mate}, {"replica": next_}
-    greeted(2)
+    greeted(greetings)
     across = [copies(own_ref.at[half], all_ref.at[me, half], to_next) for half in halves]
     beside = copies(own_ref, all_ref.at[me], to_mate)
     forwards = [copies(all_ref.at[next_, half], all_ref.at[next_, half], to_mate, False) for half in halves]
@@ -655,8 +706,8 @@
     pltpu.VMEM((ROWS, D), BF),
     pltpu.VMEM((2, 64, D), BF),
     pltpu.VMEM((2, 64, D), BF),
-    pltpu.SemaphoreType.DMA((10,)),
-    pltpu.SemaphoreType.DMA((10,)),
+    pltpu.SemaphoreType.DMA((11,)),
+    pltpu.SemaphoreType.DMA((11,)),
     pltpu.SemaphoreType.DMA((18,)),
 ]
 
@@ -702,6 +753,44 @@
         Copies(send, recv), loads, work
     )
     out_ref[...] = (hidden_ref[...] + total).astype(BF)
+
+
+def mlp_relay_kernel(
+    normed_ref, hidden_ref, x_ref, gate_hbm, up_hbm, down_hbm, next_ref, all_ref, out_ref, relayed_ref,
+    gate_w, up_w, down_w, total_ref, near_terms, part, far_part, near_sum, part_in, far_in, near_in, send, recv, local
+):
+    signal([other_section()])
+    loads = mlp_start((gate_hbm, up_hbm, down_hbm), (gate_w, up_w, down_w), local)
+
+    def work(parts):
+        rows = jnp.concatenate([all_ref[source, rows] for source, rows in parts], axis=0)
+        gate = nn(rows, gate_w[...])
+        up = nn(rows, up_w[...])
+        product = (gate * jax.nn.sigmoid(gate) * up).astype(BF)
+        return nn(product, down_w[...])
+
+    copies = Copies(send, recv)
+    total = exchange(
+        normed_ref, all_ref, total_ref, near_terms, part, far_part, near_sum, part_in, far_in, near_in,
+        copies, loads, work, 3
+    )
+    out_ref[...] = (hidden_ref[...] + total).astype(BF)
+    relay = copies(out_ref, relayed_ref, other_section())
+    relay.wait()
+    first_section = jnp.broadcast_to(lax.axis_index("section") == 0, (ROWS, D))
+    next_ref[...] = jnp.where(first_section, x_ref[...], relayed_ref[...])
+
+
+def mlp_relay(normed2, hidden, x, gate_w, up_w, down_w):
+    return pl.pallas_call(
+        mlp_relay_kernel,
+        out_shape=shaped(ROWS, D),
+        in_specs=[VMEM_SPEC] * 3 + [ANY_SPEC] * 3,
+        scratch_shapes=[pltpu.VMEM((4, ROWS, D), BF), pltpu.VMEM((ROWS, D), BF), pltpu.VMEM((ROWS, D), BF)]
+        + EXCHANGE_SCRATCH,
+        compiler_params=params(2),
+        name="mlp_relay",
+    )(normed2, hidden, x, gate_w, up_w, down_w)
 
 
 def mlp_forward(normed2, hidden, gate_w, up_w, down_w):
@@ -838,6 +927,7 @@
         z_then_y(kv_ref.at[1], *top),
         z_then_y(kv_ref.at[1], *bottom),
         copies,
+        gather_direct,
     )
     next(steps)
     projected = nn(normed, w_ref[:, :D]) + b_ref[:, :D]
@@ -850,7 +940,7 @@
     signal(neighbours(along_y, along_z))
     steps = front_work(
         x_ref, w_ref, b_ref, g_ref, cos_ref, sin_ref, normed_ref, q_ref, kv_ref,
-        Copies(send, recv), lambda: greeted(4)
+        Copies(send, recv), lambda: greeted(6)
     )
     run(steps)
 
@@ -1063,14 +1153,15 @@
 
 
 def rear_kernel(
-    dkv_ref, dq_ref, cos_ref, sin_ref, w_ref, x_ref, g_ref, dhidden_ref, dinput_ref,
-    dprojected_ref, dgain_ref, dbias_ref, total, *rest
+    dkv_ref, dq_ref, cos_ref, sin_ref, w_ref, x_ref, g_ref, dhidden_ref, cotangent_ref, next_ref,
+    dinput_ref, returned_ref, dprojected_ref, dgain_ref, dbias_ref, total, *rest
 ):
     scratch, (send, recv) = rest[:-2], rest[-2:]
     z, y, along_y, along_z = grid_place()
-    signal(neighbours(along_y, along_z))
-    greeted(4)
-    steps = kv_sums(dkv_ref, total, scratch, Copies(send, recv))
+    signal(neighbours(along_y, along_z) + [other_section()])
+    greeted(7)
+    copies = Copies(send, recv)
+    steps = kv_sums(dkv_ref, total, scratch, copies)
     next(steps)
     dnormed = rear_query(dq_ref, cos_ref, sin_ref, w_ref, dprojected_ref, dbias_ref)
     run(steps)
@@ -1078,16 +1169,22 @@
         dnormed, total, cos_ref, sin_ref, w_ref, x_ref, g_ref, dhidden_ref,
         dprojected_ref, dinput_ref, dgain_ref, dbias_ref
     )
-
-
-def rear(dkv, dq, cosine, sine, w_qkv, x, g_attn, dhidden):
+    relay = copies(dinput_ref, returned_ref, other_section())
+    relay.wait()
+    last_section = jnp.broadcast_to(lax.axis_index("section") == 1, (ROWS, D))
+    next_ref[...] = jnp.where(last_section, cotangent_ref[...], returned_ref[...])
+
+
+def rear(*operands):
     return pl.pallas_call(
         rear_kernel,
         out_shape=shaped(ROWS, D),
-        scratch_shapes=REAR_SCRATCH + [pltpu.SemaphoreType.DMA((24,)), pltpu.SemaphoreType.DMA((24,))],
+        scratch_shapes=[pltpu.VMEM((ROWS, D), BF), pltpu.VMEM((ROWS, D), BF)]
+        + REAR_SCRATCH
+        + [pltpu.SemaphoreType.DMA((25,)), pltpu.SemaphoreType.DMA((25,))],
         compiler_params=params(7),
         name="rear",
-    )(dkv, dq, cosine, sine, w_qkv, x, g_attn, dhidden)
+    )(*operands)
 
 
 TAIL_SCRATCH = [
@@ -1145,11 +1242,11 @@
     @pl.when(moves)
     def _():
         signal([target])
-        greeted(7)
+        greeted(9)
 
     @pl.when(stays)
     def _():
-        greeted(6)
+        greeted(8)
 
     copies = Copies(send, recv)
     mlp = mlp_sums(*mlp_term_refs, *mlp_sum_refs, mlp_bufs, copies)
@@ -1297,7 +1394,6 @@
 
 
 def body(inputs, cotangent, segments, w_qkv, b_qkv, w_out, w_gate, w_up, w_down, g_attn, g_mlp):
-    section = lax.axis_index("section")
     group = lax.axis_index("group")
     replica = lax.axis_index("replica")
     core = lax.rem(replica, 2)
@@ -1331,15 +1427,12 @@
         dout_all, dgate, dup, product = grads
         return (dout, dnormed2, hidden, gain2, out_w, q, kv, kseg), (normed2_all, dgate, dup, product, dout_all)
 
-    relayed, *_ = mlp_forward(normed2, hidden, gate_w, up_w, down_w)
-    relayed = lax.ppermute(relayed, "section", [(0, 1)])
-    output, kept = forward(jnp.where(section == 0, x_in, relayed))
+    output, kept = forward(mlp_relay(normed2, hidden, x_in, gate_w, up_w, down_w))
     x, normed, q, kv, context, hidden, normed2_all, gate, up = kept
     operands, _ = backward_start(cotangent_in)
     dhidden, _, dq, dkv, _ = attention_backward(*operands)
-    returned = rear(dkv, dq, cosine, sine, qkv_w, x, gain1, dhidden)
-    returned = lax.ppermute(returned, "section", [(1, 0)])
-    operands, mlp_operands = backward_start(jnp.where(section == 1, cotangent_in, returned))
+    dout = rear(dkv, dq, cosine, sine, qkv_w, x, gain1, dhidden, cotangent_in)
+    operands, mlp_operands = backward_start(dout)
     dinput, *parts = tail(*operands, *mlp_operands, cosine, sine, qkv_w, x, gain1, normed, context)
     grad_gate, grad_up, grad_down, grad_qkv, grad_out, bias, value_bias, gain1, gain2 = outputs(*parts)
     return (

time: 381 us -> 359 us (0.942); the launches traced: 373 us -> 355 us
  waiting for transfers between devices: 12.9 us -> 0 us
  starting transfers between devices: 6.5 us -> 0 us
    pallas_call x1 -> x2, Pallas kernels: 17.2 us -> 50.7 us  [the longest x1 28.2 us: mlp_relay(): pl.pallas_call(mlp_relay_kernel, out_shape=shaped(ROWS, D), in_specs=[VME...]
    pallas_call x2 -> x1, Pallas kernels: 46.1 us -> 21.1 us  [mlp_forward(): pl.pallas_call(mlp_forward_kernel, out_shape=(shaped(ROWS, D), shaped(4,...]
    ppermute x2 -> x0, waiting for transfers between devices: 12.9 us -> none  [the longest x1 7.73 us: body(): returned = lax.ppermute(returned, 'section', [(1, 0)])]
    ppermute x2 -> x0, starting transfers between devices: 6.5 us -> none  [the longest x1 5.21 us: body(): relayed = lax.ppermute(relayed, 'section', [(0, 1)])]
  transfers between devices with their start and end apart: 2 -> 0, of which waited for: 2 -> 0; matrix products, arithmetic and copies ran while one was open for 0% -> 0% of each run, Pallas kernels for 0% -> 0%
where the time goes in v1:
time: 359 us; the launch traced here: 355 us
  Pallas kernels  345 us (96%)
  local copies, waits for them, and re-layouts  5.37 us (1%)
  other arithmetic  4.02 us (1%)
    pallas_call x1, Pallas kernels, tail(): pl.pallas_call(tail_kernel, out_shape=(shaped(ROWS, D), shaped(4, 56, QUA...  98.4 us
    pallas_call x1, Pallas kernels, first(): pl.pallas_call(first_kernel, out_shape=(shaped(4, 4, *gate.shape), shaped...  76.7 us
    pallas_call x2, Pallas kernels, mlp_backward(): pl.pallas_call(mlp_backward_kernel, out_shape=(shaped(ROWS, D, dtype=F32)...  46.5 us
    pallas_call x1, Pallas kernels, mlp_relay(): pl.pallas_call(mlp_relay_kernel, out_shape=shaped(ROWS, D), in_specs=[VME...  28.2 us
    pallas_call x1, Pallas kernels, rear(): pl.pallas_call(rear_kernel, out_shape=shaped(ROWS, D), scratch_shapes=[pl...  22.4 us
    pallas_call x1, Pallas kernels, mlp_forward(): pl.pallas_call(mlp_forward_kernel, out_shape=(shaped(ROWS, D), shaped(4,...  21.1 us
    pallas_call x1, Pallas kernels, attention_backward(): local_call(attention_backward_work, 'attention_backward', ATTENTION_BACKW...  19.7 us
    pallas_call x1, Pallas kernels, front(): pl.pallas_call(front_kernel, out_shape=(shaped(ROWS, D), shaped(ROWS, D),...  15 us

profile of v1, /device:TPU:1, one launch (start us, length us, event | category | flops | bytes accessed | tf_op | source)
XLA Modules:
  0.0 355.5 jit_solution(3956089089018138383)
XLA Ops:
  0.6 0.0 copy-start
  0.7 0.8 pad_maximum_fusion
  1.5 1.4 pad_dynamic-slice_fusion.2.out
  3.0 1.5 fusion.1.qkv
  4.4 1.7 sine_multiply_fusion
  6.1 0.0 copy-done
  6.1 0.7 dynamic-slice_bitcast_fusion.down
  6.8 1.8 dynamic-slice_bitcast_fusion.1
  8.7 76.7 %first.1 = (bf16[4,4,56,1216]{3,2,1,0:T(8,128)(2,1)}, bf16[4,4,56,1216]{3,2,1,0:T(8,128)(2,1)}, bf16[4,4,80,896]{3,2,1,0:T(8,128)(2,1)}, bf16[896,1152]{1,0:T(8,...) custom-call(bf16[56,1216]{1,0:T(8,128)(2,1)} %get-tuple-element.102., ...), custom_call_target="tpu_custom_call" | custom-call | tf_op jit(solution)/shard_map/first/pallas_call | solution.py:346
  85.4 28.2 %mlp_relay.1.x_ref.refs_16_ = bf16[128,896]{1,0:T(8,128)(2,1)} custom-call(bf16[128,896]{1,0:T(8,128)(2,1)} %get-tuple-element.55.normed_ref, f32[128,896]{1,0:T(8,128)} %get-tuple-element.56.hidden_ref, bf16[128,896]{1,0:T(8,128)(2,1)} %bitcast.34, bf16[896,1216]{1,0:T(8,128)(2,1)} %bitcast.22, bf16[896,1216]{1,0:T(8,128)(2,1)} %bitcast.26, ...), custom_call_target="tpu_custom_call" | custom-call | tf_op jit(solution)/shard_map/mlp_relay/pallas_call | solution.py:785
  113.6 15.0 %front.1 = (bf16[128,896]{1,0:T(8,128)(2,1)}, bf16[128,896]{1,0:T(8,128)(2,1)}, bf16[2,4,4,64,256]{4,3,2,1,0:T(8,128)(2,1)}) custom-call(bf16[128,896]{1,0:T(8,128)(2,1)} %mlp_relay.1.x_ref.refs_16_, bf16[896,1152]{1,0:T(8,128)(2,1)} %get-tuple-element.60.w_ref.refs_15_, f32[1,1152]{1,0:T(1,128)} %get-tuple-element.61.b_ref, ...), custom_call_target="tpu_custom_call" | custom-call | tf_op jit(solution)/shard_map/front/pallas_call | solution.py:949
  128.6 13.2 %attention.1 = (bf16[128,896]{1,0:T(8,128)(2,1)}, f32[128,896]{1,0:T(8,128)}, bf16[128,896]{1,0:T(8,128)(2,1)}) custom-call(bf16[128,896]{1,0:T(8,128)(2,1)} %mlp_relay.1.x_ref.refs_16_, bf16[128,896]{1,0:T(8,128)(2,1)} %get-tuple-element.63.q_ref.refs_5_, bf16[2,4,4,64,256]{4,3,2,1,0:T(8,128)(2,1)} %get-tuple-element.64.kv_ref.refs_6_, s32[1,2048]{1,0:T(1,128)} %refs_7_.1, ...), custom_call_target="tpu_custom_call" | custom-call | tf_op jit(solution)/shard_map/attention/pallas_call | solution.py:1043
  141.8 21.1 %mlp_forward.1 = (bf16[128,896]{1,0:T(8,128)(2,1)}, bf16[4,128,896]{2,1,0:T(8,128)(2,1)}, bf16[4,128,1216]{2,1,0:T(8,128)(2,1)}, bf16[4,128,1216]{2,1,0:T(8,128)(2,1)}) custom-call(bf16[128,896]{1,0:T(8,128)(2,1)} %get-tuple-element.67.normed_ref, f32[128,896]{1,0:T(8,128)} %get-tuple-element.68.hidden_ref.refs_2_, bf16[896,1216]{1,0:T(8,128)(2,1)} %bitcast.23, ...), custom_call_target="tpu_custom_call" | custom-call | tf_op jit(solution)/shard_map/mlp_forward/pallas_call | solution.py:797
  162.9 22.8 %mlp_backward.2 = (f32[128,896]{1,0:T(8,128)}, bf16[4,128,896]{2,1,0:T(8,128)(2,1)}, bf16[4,128,1216]{2,1,0:T(8,128)(2,1)}, bf16[4,128,1216]{2,1,0:T(8,128)(2,1)}, bf16[4,128,1216]{2,1,0:T(8,128)(2,1)}) custom-call(bf16[128,896]{1,0:T(8,128)(2,1)} %bitcast.30, bf16[4,128,1216]{2,1,0:T(8,128)(2,1)} %get-tuple-element.70.gate_ref, ...), custom_call_target="tpu_custom_call" | custom-call | tf_op jit(solution)/shard_map/mlp_backward/pallas_call | solution.py:844
  185.8 19.7 %attention_backward.1 = (f32[128,896]{1,0:T(8,128)}, bf16[128,896]{1,0:T(8,128)(2,1)}, f32[128,896]{1,0:T(8,128)}, bf16[2,4,4,64,256]{4,3,2,1,0:T(8,128)(2,1)}, f32[1,896]{1,0:T(1,128)}) custom-call(bf16[128,896]{1,0:T(8,128)(2,1)} %bitcast.31, f32[128,896]{1,0:T(8,128)} %get-tuple-element.72.dnormed_ref, f32[128,896]{1,0:T(8,128)} %get-tuple-element.68.hidden_ref.refs_2_, ...), custom_call_target="tpu_custom_call" | custom-call | tf_op jit(solution)/shard_map/attention_backward/pallas_call | solution.py:1122
  205.4 22.4 %rear.1.dout_ref.refs_0_ = bf16[128,896]{1,0:T(8,128)(2,1)} custom-call(bf16[2,4,4,64,256]{4,3,2,1,0:T(8,128)(2,1)} %get-tuple-element.73.dkv_ref, f32[128,896]{1,0:T(8,128)} %get-tuple-element.74.dq_ref, f32[128,128]{1,0:T(8,128)} %get-tuple-element.100.cos_ref.refs_13_, f32[128,128]{1,0:T(8,128)} %get-tuple-element.99.sin_ref.refs_14_, ...), custom_call_target="tpu_custom_call" | custom-call | tf_op jit(solution)/shard_map/rear/pallas_call | solution.py:1179
  227.9 23.6 %mlp_backward.3 = (f32[128,896]{1,0:T(8,128)}, bf16[4,128,896]{2,1,0:T(8,128)(2,1)}, bf16[4,128,1216]{2,1,0:T(8,128)(2,1)}, bf16[4,128,1216]{2,1,0:T(8,128)(2,1)}, bf16[4,128,1216]{2,1,0:T(8,128)(2,1)}) custom-call(bf16[128,896]{1,0:T(8,128)(2,1)} %rear.1.dout_ref.refs_0_, bf16[4,128,1216]{2,1,0:T(8,128)(2,1)} %get-tuple-element.70.gate_ref, ...), custom_call_target="tpu_custom_call" | custom-call | tf_op jit(solution)/shard_map/mlp_backward/pallas_call | solution.py:844
  251.5 98.4 %tail.1 = (bf16[128,896]{1,0:T(8,128)(2,1)}, bf16[4,56,1216]{2,1,0:T(8,128)(2,1)}, bf16[4,56,1216]{2,1,0:T(8,128)(2,1)}, bf16[4,80,896]{2,1,0:T(8,128)(2,1)}, f3...) custom-call(bf16[128,896]{1,0:T(8,128)(2,1)} %rear.1.dout_ref.refs_0_, f32[128,896]{1,0:T(8,128)} %get-tuple-element.76.refs_1_, ...), custom_call_target="tpu_custom_call" | custom-call | tf_op jit(solution)/shard_map/tail/pallas_call | solution.py:1360
  350.0 0.0 copy-start.1
  350.0 0.0 copy-start.2
  350.0 3.7 %outputs.1 = (f32[56,4864]{1,0:T(8,128)}, f32[56,4864]{1,0:T(8,128)}, f32[304,896]{1,0:T(8,128)}, f32[56,1152]{1,0:T(8,128)}, f32[56,896]{1,0:T(8,128)}, /*index...) custom-call(bf16[4,56,1216]{2,1,0:T(8,128)(2,1)} %get-tuple-element.85.gate, ...), custom_call_target="tpu_custom_call" | custom-call | tf_op jit(solution)/shard_map/outputs/pallas_call | solution.py:881
  353.7 0.0 copy-done.1
  353.7 0.7 copy.26
  354.4 0.0 copy-done.2
  354.4 0.7 copy.27
  (4 shorter events, 0.0 us)
Async XLA Ops:
  0.6 5.5 %copy-start = (bf16[1,304,896]{2,1,0:T(8,128)(2,1)S(1)}, bf16[1,304,896]{2,1,0:T(8,128)(2,1)}, u32[]{:S(2)}) copy-start(bf16[1,304,896]{2,1,0:T(8,128)(2,1)} %param.21) | copy-start | bytes 1634308
  350.0 3.7 %copy-start.1 = (bf16[128,896]{1,0:T(8,128)(2,1)S(1)}, bf16[128,896]{1,0:T(8,128)(2,1)}, u32[]{:S(2)}) copy-start(bf16[128,896]{1,0:T(8,128)(2,1)} %get-tuple-element.69) | copy-start | bytes 688132
  350.0 4.4 %copy-start.2 = (bf16[128,896]{1,0:T(8,128)(2,1)S(1)}, bf16[128,896]{1,0:T(8,128)(2,1)}, u32[]{:S(2)}) copy-start(bf16[128,896]{1,0:T(8,128)(2,1)} %get-tuple-element.84) | copy-start | bytes 688132
